TPU v7x, 32 devices: a whole 2x2x4 slice. The times are simulated.
32 devices in a mesh: rows: 8 (over z, x), cols: 4 (over y, core).
Axes of the slice: x: 2, y: 2, z: 4, core: 2. Of those that a mesh axis runs over, the one named last changes fastest.
Arguments:
- kernel: float32 [16384, 16384], P('rows', 'cols'), may hold values from 0 to 2, as said below
- row_block: int32 [256], P('rows'), may hold values from 0 to 255, as said below
- panel_order: int32 [2], replicated, may hold values from 0 to 63, as said below
- samples: float32 [16384, 512], P('rows', 'cols'), may hold values from -6 to 6
Outputs:
- trailing: float32 [16384, 16384], P('rows', 'cols')
- factor: float32 [16384, 512], P('rows')
- solved: float32 [512, 512], P(None, 'cols')
- reduced_samples: float32 [16384, 512], P('rows', 'cols')
Inputs may be any that keep to these rules, and one draw needn't show every extreme that they name: `row_block`: the stored row blocks of rows index i (stored blocks i * 32 to (i + 1) * 32 - 1) hold the global row blocks i + t * 8, t = 0 .. 31, each once, in some order. `panel_order`: the entries are distinct, and one of them is 63. `kernel`: in global row order the matrix is symmetric and positive definite, its smallest eigenvalue 0.25 or more.
All inputs are finite; a program needn't handle non-finite values.
Results may differ from a plain program's by a relative error of at most 0.0003.
Values sent between devices are 32-bit elements; how exact they have to be, the bound alone decides.
A program may use at most 320 MiB of HBM per device.

v0:
```python
import jax
import jax.numpy as jnp
from jax import lax
from jax.sharding import PartitionSpec as P

PW = 256
PANELS = 2


EXACT = lax.Precision.HIGHEST


def broadcast(block, axis, owner):
    block = jnp.where(lax.axis_index(axis) == owner, block, jnp.zeros_like(block))
    return lax.psum(block, axis)


def times_transposed(left_side, right_side):
    return lax.dot_general(
        left_side,
        right_side,
        (((1,), (1,)), ((), ())),
        precision=EXACT,
        preferred_element_type=jnp.float32,
    )


def matmul_plain(left_side, right_side):
    return jnp.dot(left_side, right_side, precision=EXACT, preferred_element_type=jnp.float32)


def stored_order(array, restore, blocks_here):
    width_here = array.shape[1]
    return jnp.take(array.reshape(blocks_here, -1, width_here), restore, axis=0).reshape(
        array.shape
    )


def on_device(kernel, row_block, panel_order, samples):
    rows_count = lax.axis_size("rows")
    cols_count = lax.axis_size("cols")
    cols_place = lax.axis_index("cols")
    blocks_here = row_block.shape[0]
    local_rows, local_cols = kernel.shape
    block_rows = local_rows // blocks_here
    per_panel = PW // block_rows
    share = blocks_here // cols_count
    right_cols = samples.shape[1]
    ranking = jnp.argsort(row_block)
    restore = jnp.argsort(ranking)
    sorted_blocks = jnp.take(row_block, ranking)
    trailing_work = jnp.take(
        kernel.reshape(blocks_here, block_rows, local_cols), ranking, axis=0
    ).reshape(local_rows, local_cols)
    right_side = jnp.take(
        samples.reshape(blocks_here, block_rows, right_cols), ranking, axis=0
    ).reshape(local_rows, right_cols)
    identity = jnp.eye(PW, dtype=jnp.float32)
    factors = []
    solutions = []
    for panel_step in range(PANELS):
        panel_start = panel_order[panel_step] * PW
        column_owner = panel_start // local_cols
        offset = panel_start - column_owner * local_cols
        own_columns = lax.dynamic_slice_in_dim(trailing_work, offset, PW, 1)
        columns = broadcast(own_columns, "cols", column_owner)
        first_block = panel_order[panel_step] * per_panel
        wanted = first_block + jnp.arange(per_panel, dtype=jnp.int32)
        chooser = (wanted[:, None] == sorted_blocks[None, :]).astype(jnp.float32)
        diag_part = jnp.einsum(
            "ot,trp->orp", chooser, columns.reshape(blocks_here, block_rows, PW), precision=EXACT
        ).reshape(PW, PW)
        right_part = jnp.einsum(
            "ot,trp->orp",
            chooser,
            right_side.reshape(blocks_here, block_rows, right_cols),
            precision=EXACT,
        ).reshape(PW, right_cols)
        diagonal, panel_right = lax.psum((diag_part, right_part), "rows")
        lower_factor = jnp.linalg.cholesky(diagonal)
        inverse = jax.scipy.linalg.solve_triangular(lower_factor, identity, lower=True)
        factor_own = times_transposed(columns, inverse)
        solved_now = matmul_plain(inverse, panel_right)
        right_side = right_side - matmul_plain(factor_own, solved_now)
        my_piece = lax.dynamic_slice_in_dim(
            factor_own, cols_place * share * block_rows, share * block_rows, 0
        )
        spread = times_transposed(factor_own, lax.all_gather(my_piece, "rows", axis=0, tiled=True))
        update = (
            spread.reshape(local_rows, rows_count, share, block_rows)
            .transpose(0, 2, 1, 3)
            .reshape(local_rows, local_cols)
        )
        trailing_work = trailing_work - update
        factors.append(factor_own)
        solutions.append(solved_now)
    factor_all = jnp.concatenate(factors, 1)
    return (
        stored_order(trailing_work, restore, blocks_here),
        stored_order(factor_all, restore, blocks_here),
        jnp.concatenate(solutions, 0),
        stored_order(right_side, restore, blocks_here),
    )


def solution(mesh):
    in_specs = (P("rows", "cols"), P("rows"), P(), P("rows", "cols"))
    out_specs = (P("rows", "cols"), P("rows", None), P(None, "cols"), P("rows", "cols"))
    return jax.shard_map(
        on_device, mesh=mesh, in_specs=in_specs, out_specs=out_specs, check_vma=False
    )
```

profile of v0, /device:TPU:0, one launch (start us, length us, event | category | flops | bytes accessed | tf_op | source)
XLA Modules:
  0.0 968.5 jit_solution(1337913702325062290)
XLA Ops:
  7.2 1.4 fusion.52
  9.3 2.3 sort.31
  11.6 1.6 sort.32
  15.1 23.0 %gather_fusion.2 = f32[32,64,4096]{2,1,0:T(8,128)} fusion(f32[32,64,4096]{2,1,0:T(8,128)} %bitcast.123, s32[1024]{0:T(1024)S(1)} %pad_clamp_fusion.1), kind=kCustom, calls=%fused_computation.clone | custom fusion | bytes 67108992 | tf_op jit(solution)/shard_map/jit(_take)/gather | solution.py:52
  38.1 12.6 %broadcast_select_fusion.1 = f32[32,64,4096]{2,1,0:T(8,128)S(1)} fusion(f32[32,64,4096]{2,1,0:T(8,128)} %gather_fusion.2, pred[32]{0:T(512)(128)(4,1)S(1)} %get-tuple-element.49), kind=kLoop, calls=%fused_computation.12 | loop fusion | flops 8388608 | bytes 67108896 | tf_op jit(solution)/shard_map/jit(_take)/select_n | solution.py:52
  50.7 11.1 %copy-done.2 = f32[32,64,4096]{2,1,0:T(8,128)} copy-done((f32[32,64,4096]{2,1,0:T(8,128)}, f32[32,64,4096]{2,1,0:T(8,128)S(1)}, u32[]{:S(2)}) %copy-start.2) | copy-done | bytes 33554456
  61.8 1.6 dynamic-slice_select_fusion
  66.6 51.0 %all-reduce.8.cloned.1.call-done = f32[2048,256]{1,0:T(8,128)} async-done(((f32[2048,256]{1,0:T(8,128)}), f32[2048,256]{1,0:T(8,128)}) %all-reduce.8.cloned.1.call-update) | async-done | bytes 2097168 | tf_op jit(solution)/shard_map/psum | solution.py:15
  117.7 3.4 fusion.3
  122.3 71.5 %all-reduce.14.cloned.1.call-done = (f32[256,256]{0,1:T(8,128)}, f32[256,128]{1,0:T(8,128)}) async-done(((f32[256,256]{0,1:T(8,128)}, f32[256,128]{1,0:T(8,128)}), (f32[256,256]{0,1:T(8,128)}, f32[256,128]{1,0:T(8,128)})) %all-reduce.14.cloned.1.call-update) | async-done | bytes 393232 | tf_op jit(solution)/shard_map/psum | solution.py:79
  195.8 11.7 %cholesky.130 = f32[128,128]{1,0:T(8,128)S(1)} custom-call(f32[128,128]{1,0:T(8,128)S(1)} %cholesky.194), custom_call_target="Cholesky" | custom-call | tf_op jit(solution)/shard_map/jit(cholesky)/cholesky | solution.py:80
  208.2 9.8 %custom-call.13 = f32[1,128,128]{1,2,0:T(8,128)S(1)} custom-call(f32[1,128,128]{2,1,0:T(8,128)S(1)} %get-tuple-element.61), custom_call_target="InvertDiagBlocksLowerTriangular" | custom-call | tf_op jit(solution)/shard_map/jit(cholesky)/cholesky | solution.py:80
  218.5 11.7 %cholesky.147 = f32[128,128]{1,0:T(8,128)S(1)} custom-call(f32[128,128]{1,0:T(8,128)S(1)} %convolution_subtract_fusion.5), custom_call_target="Cholesky" | custom-call | tf_op jit(solution)/shard_map/jit(cholesky)/cholesky | solution.py:80
  232.3 4.2 while.4
  233.2 1.4 bitcast_dynamic-update-slice_fusion.4
  236.6 19.7 %custom-call.14 = f32[2,128,128]{1,2,0:T(8,128)S(1)} custom-call(f32[2,128,128]{2,1,0:T(8,128)S(1)} %get-tuple-element.26), custom_call_target="InvertDiagBlocksLowerTriangular" | custom-call | tf_op jit(solution)/shard_map/jit(_solve_triangular)/triangular_solve | solution.py:81
  257.8 3.6 fusion.15
  263.0 71.9 %all-gather.3.cloned.1.call-done = f32[4096,256]{0,1:T(8,128)} async-done(((f32[512,256]{0,1:T(8,128)}), f32[4096,256]{0,1:T(8,128)}) %all-gather.3.cloned.1.call-update) | async-done | bytes 4194320 | tf_op jit(solution)/shard_map/all_gather | solution.py:88
  334.9 31.8 %fusion.53 = f32[2048,4096]{0,1:T(8,128)} fusion(f32[2048,256]{0,1:T(8,128)S(1)} %fusion.15, f32[4096,256]{0,1:T(8,128)} %all-gather.3.cloned.1.call-done), kind=kOutput, calls=%fused_computation.120 | convolution fusion | flops 25769803776 | bytes 39845888 | tf_op jit(solution)/shard_map/dot_general | solution.py:19
  366.7 12.0 %copy.21 = f32[2048,8,8,64]{0,3,2,1:T(8,128)S(1)} copy(f32[2048,8,8,64]{0,3,1,2:T(8,128)} %bitcast.117) | data formatting | bytes 67108864 | tf_op jit(solution)/shard_map/transpose | solution.py:91
  378.7 1.5 constant_dynamic-slice_fusion.3
  380.2 2.9 copy.36
  383.1 3.8 fusion
  389.4 3.5 convolution_subtract_fusion.1
  395.6 41.1 %all-reduce.10.cloned.1.call-done = f32[2048,256]{1,0:T(8,128)} async-done(((f32[2048,256]{1,0:T(8,128)}), f32[2048,256]{1,0:T(8,128)}) %all-reduce.10.cloned.1.call-update) | async-done | bytes 2097168 | tf_op jit(solution)/shard_map/psum | solution.py:15
  436.7 3.4 fusion.1
  441.3 71.5 %all-reduce.12.cloned.1.call-done = (f32[256,256]{0,1:T(8,128)}, f32[256,128]{1,0:T(8,128)}) async-done(((f32[256,256]{0,1:T(8,128)}, f32[256,128]{1,0:T(8,128)}), (f32[256,256]{0,1:T(8,128)}, f32[256,128]{1,0:T(8,128)})) %all-reduce.12.cloned.1.call-update) | async-done | bytes 393232 | tf_op jit(solution)/shard_map/psum | solution.py:79
  514.9 11.7 %cholesky.164 = f32[128,128]{1,0:T(8,128)S(1)} custom-call(f32[128,128]{1,0:T(8,128)S(1)} %cholesky.197), custom_call_target="Cholesky" | custom-call | tf_op jit(solution)/shard_map/jit(cholesky)/cholesky | solution.py:80
  527.3 9.8 %custom-call.15 = f32[1,128,128]{1,2,0:T(8,128)S(1)} custom-call(f32[1,128,128]{2,1,0:T(8,128)S(1)} %get-tuple-element.57), custom_call_target="InvertDiagBlocksLowerTriangular" | custom-call | tf_op jit(solution)/shard_map/jit(cholesky)/cholesky | solution.py:80
  537.6 11.7 %cholesky.181 = f32[128,128]{1,0:T(8,128)S(1)} custom-call(f32[128,128]{1,0:T(8,128)S(1)} %convolution_subtract_fusion.4), custom_call_target="Cholesky" | custom-call | tf_op jit(solution)/shard_map/jit(cholesky)/cholesky | solution.py:80
  551.4 4.2 while.5
  554.2 1.4 bitcast_dynamic-update-slice_fusion.5
  555.6 19.7 %custom-call.16 = f32[2,128,128]{1,2,0:T(8,128)S(1)} custom-call(f32[2,128,128]{2,1,0:T(8,128)S(1)} %get-tuple-element.27), custom_call_target="InvertDiagBlocksLowerTriangular" | custom-call | tf_op jit(solution)/shard_map/jit(_solve_triangular)/triangular_solve | solution.py:81
  576.2 3.6 fusion.13
  582.2 59.6 %copy.20 = f32[2048,8,8,64]{3,2,1,0:T(8,128)} copy(f32[2048,8,8,64]{0,3,1,2:T(8,128)} %bitcast.118) | data formatting | bytes 67108864 | tf_op jit(solution)/shard_map/transpose | solution.py:91
  641.8 54.7 %reshape.133 = f32[32,64,4096]{2,1,0:T(8,128)} reshape(f32[2048,8,8,64]{3,2,1,0:T(8,128)} %copy.20) | data formatting | bytes 67108864 | tf_op jit(solution)/shard_map/reshape | solution.py:92
  696.5 4.0 pad_maximum_fusion
  700.5 5.7 copy.29
  707.6 4.4 convolution_subtract_fusion
  712.0 1.8 gather_fusion.5
  713.8 5.1 gather_fusion.1
  720.7 3.8 bitcast_select_fusion
  724.6 31.7 %fusion.54 = f32[2048,4096]{0,1:T(8,128)} fusion(f32[2048,256]{0,1:T(8,128)S(1)} %copy-done.4, f32[4096,256]{0,1:T(8,128)} %all-gather.5.cloned.1.call-done), kind=kOutput, calls=%fused_computation.121 | convolution fusion | flops 25769803776 | bytes 39845888 | tf_op jit(solution)/shard_map/dot_general | solution.py:19
  756.3 59.8 %copy.28 = f32[2048,8,8,64]{3,2,1,0:T(8,128)} copy(f32[2048,8,8,64]{0,3,1,2:T(8,128)} %bitcast.119) | data formatting | bytes 67108864 | tf_op jit(solution)/shard_map/transpose | solution.py:91
  816.1 54.7 %reshape.138 = f32[32,64,4096]{2,1,0:T(8,128)} reshape(f32[2048,8,8,64]{3,2,1,0:T(8,128)} %copy.28) | data formatting | bytes 67108864 | tf_op jit(solution)/shard_map/reshape | solution.py:92
  870.8 44.0 %subtract_subtract_fusion = f32[32,64,4096]{2,1,0:T(8,128)} fusion(f32[32,64,4096]{2,1,0:T(8,128)} %reshape.138, f32[32,64,4096]{2,1,0:T(8,128)} %reshape.133, f32[32,64,4096]{2,1,0:T(8,128)} %gather_fusion.2, pred[32]{0:T(512)(128)(4,1)S(1)} %copy-done.11), kind=kLoop, calls=%fused_computation.10 | loop fusion | flops 25165824 | bytes 134217760 | tf_op jit(solution)/shard_map/sub | solution.py:94
  914.8 22.8 %gather_fusion.3 = f32[32,64,4096]{2,1,0:T(8,128)} fusion(f32[32,64,4096]{2,1,0:T(8,128)} %subtract_subtract_fusion, s32[1024]{0:T(1024)S(1)} %pad_clamp_fusion), kind=kCustom, calls=%fused_computation.2.clone | custom fusion | bytes 67108992 | tf_op jit(solution)/shard_map/jit(_take)/gather | solution.py:34
  937.6 23.6 %broadcast_select_fusion = f32[32,64,4096]{2,1,0:T(8,128)} fusion(f32[32,64,4096]{2,1,0:T(8,128)} %gather_fusion.3, pred[32]{0:T(512)(128)(4,1)S(1)} %compare_and_fusion), kind=kLoop, calls=%fused_computation.11 | loop fusion | flops 8388608 | bytes 67108896 | tf_op jit(solution)/shard_map/jit(_take)/select_n | solution.py:34
  (111 shorter events, 33.2 us)
Async XLA Ops:
  7.2 57.0 %copy-start = (f32[2048,128]{1,0:T(8,128)S(1)}, f32[2048,128]{1,0:T(8,128)}, u32[]{:S(2)}) copy-start(f32[2048,128]{1,0:T(8,128)} %param.14) | copy-start | bytes 3145732
  7.2 110.5 %all-reduce.8.cloned.1.call-start = ((), (), s32[]{:S(2)}) async-start(), calls=%async_computation | async-start | bytes 4194304 | tf_op jit(solution)/shard_map/psum | solution.py:15
  13.2 0.5 copy-start.12
  15.1 49.7 %copy-start.10 = (pred[32]{0:T(512)(128)(4,1)}, pred[32]{0:T(512)(128)(4,1)S(1)}, u32[]{:S(2)}) copy-start(pred[32]{0:T(512)(128)(4,1)S(1)} %get-tuple-element.49) | copy-start | bytes 100
  50.7 11.1 %copy-start.2 = (f32[32,64,4096]{2,1,0:T(8,128)}, f32[32,64,4096]{2,1,0:T(8,128)S(1)}, u32[]{:S(2)}) copy-start(f32[32,64,4096]{2,1,0:T(8,128)S(1)} %broadcast_select_fusion.1) | copy-start | bytes 100663296
  63.4 130.3 %all-reduce.14.cloned.1.call-start = ((), (), s32[]{:S(2)}) async-start(), calls=%async_computation.5 | async-start | bytes 786432 | tf_op jit(solution)/shard_map/psum | solution.py:79
  122.0 212.9 %all-gather.3.cloned.1.call-start = ((), (), s32[]{:S(2)}) async-start(), calls=%async_computation.1 | async-start | bytes 4718592 | tf_op jit(solution)/shard_map/all_gather | solution.py:88
  257.2 0.7 copy-start.7
  262.3 174.5 %all-reduce.10.cloned.1.call-start = ((), (), s32[]{:S(2)}) async-start(), calls=%async_computation.2 | async-start | bytes 4194304 | tf_op jit(solution)/shard_map/psum | solution.py:15
  386.9 125.9 %all-reduce.12.cloned.1.call-start = ((), (), s32[]{:S(2)}) async-start(), calls=%async_computation.4 | async-start | bytes 786432 | tf_op jit(solution)/shard_map/psum | solution.py:79
  389.4 5.6 copy-start.8
  392.9 1.0 copy-start.5
  441.1 283.5 %all-gather.5.cloned.1.call-start = ((), (), s32[]{:S(2)}) async-start(), calls=%async_computation.3 | async-start | bytes 4718592 | tf_op jit(solution)/shard_map/all_gather | solution.py:88
  551.3 30.7 %copy-start.13 = (s32[32]{0:T(128)S(1)}, s32[32]{0:T(128)}, u32[]{:S(2)}) copy-start(s32[32]{0:T(128)} %copy-done.12) | copy-start | bytes 388
  579.8 1.3 copy-start.3
  700.5 7.0 copy-start.4
  700.5 7.0 copy-start.6
  713.8 5.1 copy-start.9
  816.1 54.7 %copy-start.11 = (pred[32]{0:T(512)(128)(4,1)S(1)}, pred[32]{0:T(512)(128)(4,1)}, u32[]{:S(2)}) copy-start(pred[32]{0:T(512)(128)(4,1)} %copy-done.10) | copy-start | bytes 100
  937.6 23.6 %copy-start.1 = (f32[2048,128]{1,0:T(8,128)S(1)}, f32[2048,128]{1,0:T(8,128)}, u32[]{:S(2)}) copy-start(f32[2048,128]{1,0:T(8,128)} %param.14) | copy-start | bytes 3145732
Sparse Core Ops, SparseCore 0:
  63.5 54.0 all-reduce.7
  122.1 71.5 all-reduce.13
  262.4 72.4 all-gather.2
  387.0 49.6 all-reduce.9
  441.2 71.5 all-reduce.11
  582.1 72.4 all-gather.4
where the time goes:
time: 978 us; the launch traced here: 969 us
  local copies, waits for them, and re-layouts  337 us (34%)
  waiting for transfers between devices  307 us (31%)
  other arithmetic  210 us (21%)
  matrix products  93 us (10%)
  between operations  20.3 us (2%)
    psum x2, waiting for transfers between devices, on_device(): diagonal, panel_right = lax.psum((diag_part, right_part), 'rows')  143 us
    transpose x3, local copies, waits for them, and re-layouts, on_device(): update = spread.reshape(local_rows, rows_count, share, block_rows).transp...  131 us
    reshape x2, local copies, waits for them, and re-layouts, on_device(): update = spread.reshape(local_rows, rows_count, share, block_rows).transp...  109 us
    psum x2, waiting for transfers between devices, broadcast(): return lax.psum(block, axis)  92.1 us
    all_gather x2, waiting for transfers between devices, on_device(): lax.all_gather(my_piece, 'rows', axis=0, tiled=True)  71.9 us
    dot_general x4, matrix products, times_transposed(): lax.dot_general(left_side, right_side, (((1,), (1,)), ((), ())), precisio...  70.8 us
    another operation x14, other arithmetic, on_device(): lower_factor = jnp.linalg.cholesky(diagonal)  69.2 us
    sub x1, other arithmetic, on_device(): trailing_work = trailing_work - update  44 us
  transfers between devices with their start and end apart: 6, of which 5 were waited for; matrix products, arithmetic and copies ran while one was open for 16% of the time, Pallas kernels for 0%

commit v1 on v0

v1 whole, which is shorter than its diff:
```python
import functools

import jax
import jax.numpy as jnp
from jax import lax
from jax.experimental import pallas as pl
from jax.experimental.pallas import tpu as pltpu
from jax.sharding import PartitionSpec as P

PW = 256
PANELS = 2
WIDE = PW * PANELS
SUB = 128
STRIP = 8

EXACT = lax.Precision.HIGHEST


def eliminate(block):
    strips = [block[s * STRIP : (s + 1) * STRIP, :] for s in range(SUB // STRIP)]
    row_id = lax.broadcasted_iota(jnp.int32, (STRIP, SUB), 0)
    lane_id = lax.broadcasted_iota(jnp.int32, (STRIP, SUB), 1)
    right = [
        jnp.where(lane_id == row_id + s * STRIP, 1.0, 0.0).astype(jnp.float32)
        for s in range(SUB // STRIP)
    ]
    below = lax.broadcasted_iota(jnp.int32, (STRIP, 1), 0)
    pivots = [jnp.zeros((STRIP, 1), jnp.float32) for s in range(SUB // STRIP)]
    for col in range(SUB):
        home, place = divmod(col, STRIP)
        row_left = strips[home][place : place + 1, :]
        row_right = right[home][place : place + 1, :]
        pivot = row_left[:, col : col + 1]
        scale = 1.0 / pivot
        pivots[home] = jnp.where(below == place, pivot, pivots[home])
        scaled_left = row_left * scale
        scaled_right = row_right * scale
        for s in range(home, SUB // STRIP):
            if s == home and place == STRIP - 1:
                continue
            ratio = strips[s][:, col : col + 1]
            if s == home:
                ratio = jnp.where(below > place, ratio, 0.0)
            strips[s] = strips[s] - ratio * scaled_left
            right[s] = right[s] - ratio * scaled_right
    return jnp.concatenate(
        [right[s] * lax.rsqrt(pivots[s]) for s in range(SUB // STRIP)], axis=0
    )


def invert_kernel(diag_ref, out_ref, work):
    count = WIDE // SUB
    work[:, :WIDE] = diag_ref[...]
    rows = lax.broadcasted_iota(jnp.int32, (WIDE, WIDE), 0)
    lanes = lax.broadcasted_iota(jnp.int32, (WIDE, WIDE), 1)
    work[:, WIDE:] = jnp.where(rows == lanes, 1.0, 0.0).astype(jnp.float32)

    def step(k, carry):
        here = pl.ds(pl.multiple_of(k * SUB, SUB), SUB)
        inverse = eliminate(work[here, here])
        scaled = jnp.dot(
            inverse, work[here, :], precision=EXACT, preferred_element_type=jnp.float32
        )
        work[here, :] = scaled
        for i in range(1, count):

            @pl.when(i > k)
            def _():
                left = work[here, i * SUB : (i + 1) * SUB]
                work[i * SUB : (i + 1) * SUB, :] -= lax.dot_general(
                    left,
                    work[here, :],
                    (((0,), (0,)), ((), ())),
                    precision=EXACT,
                    preferred_element_type=jnp.float32,
                )

        return carry

    lax.fori_loop(0, count, step, 0)
    out_ref[...] = work[:, WIDE:]


def invert(diagonal):
    return pl.pallas_call(
        invert_kernel,
        out_shape=jax.ShapeDtypeStruct((WIDE, WIDE), jnp.float32),
        in_specs=[pl.BlockSpec(memory_space=pltpu.VMEM)],
        out_specs=pl.BlockSpec(memory_space=pltpu.VMEM),
        scratch_shapes=[pltpu.VMEM((WIDE, 2 * WIDE), jnp.float32)],
        compiler_params=pltpu.CompilerParams(vmem_limit_bytes=32 * 1024 * 1024),
        name="invert",
    )(diagonal)


def halves(value):
    high = value.astype(jnp.bfloat16)
    low = (value - high.astype(jnp.float32)).astype(jnp.bfloat16)
    return high, low


def times_transposed(left, right):
    return lax.dot_general(
        left,
        right,
        (((1,), (1,)), ((), ())),
        precision=EXACT,
        preferred_element_type=jnp.float32,
    )


def split_product(left, right):
    def one(a, b):
        return lax.dot_general(
            a, b, (((1,), (1,)), ((), ())), preferred_element_type=jnp.float32
        )

    return one(left[0], right[0]) + (one(left[0], right[1]) + one(left[1], right[0]))


def update_kernel(
    inverse_ref, wanted_ref, cols_ref, own_ref, kernel_ref, samples_ref,
    trailing_ref, factor_ref, solved_ref, reduced_ref,
    own_high, own_low, cols_high, cols_low,
):
    j = pl.program_id(0)
    i = pl.program_id(1)
    tile = kernel_ref.shape[0]
    at = pl.ds(pl.multiple_of(i * tile, tile), tile)

    @pl.when((i == 0) & (j == 0))
    def _():
        solved_ref[...] = jnp.dot(
            inverse_ref[...], wanted_ref[...], precision=EXACT, preferred_element_type=jnp.float32
        )

    @pl.when(i == 0)
    def _():
        high, low = halves(times_transposed(cols_ref[...], inverse_ref[...]))
        cols_high[...] = high
        cols_low[...] = low

    @pl.when(j == 0)
    def _():
        factor = times_transposed(own_ref[...], inverse_ref[...])
        factor_ref[...] = factor
        high, low = halves(factor)
        own_high[at, :] = high
        own_low[at, :] = low
        reduced_ref[...] = samples_ref[...] - jnp.dot(
            factor, solved_ref[...], precision=EXACT, preferred_element_type=jnp.float32
        )

    trailing_ref[...] = kernel_ref[...] - split_product(
        (own_high[at, :], own_low[at, :]), (cols_high[...], cols_low[...])
    )


def update(inverse, wanted, columns, own, kernel, samples):
    rows, width = kernel.shape
    right = samples.shape[1]
    tile = min(512, rows)
    span = min(1024, width)
    steps = rows // tile

    def first(j, i):
        return (jnp.where(j == 0, i, steps - 1), 0)

    return pl.pallas_call(
        update_kernel,
        grid=(width // span, steps),
        in_specs=[
            pl.BlockSpec((WIDE, WIDE), lambda j, i: (0, 0)),
            pl.BlockSpec((WIDE, right), lambda j, i: (0, 0)),
            pl.BlockSpec((span, WIDE), lambda j, i: (j, 0)),
            pl.BlockSpec((tile, WIDE), first),
            pl.BlockSpec((tile, span), lambda j, i: (i, j)),
            pl.BlockSpec((tile, right), first),
        ],
        out_specs=[
            pl.BlockSpec((tile, span), lambda j, i: (i, j)),
            pl.BlockSpec((tile, WIDE), first),
            pl.BlockSpec((WIDE, right), lambda j, i: (0, 0)),
            pl.BlockSpec((tile, right), first),
        ],
        out_shape=[
            jax.ShapeDtypeStruct((rows, width), jnp.float32),
            jax.ShapeDtypeStruct((rows, WIDE), jnp.float32),
            jax.ShapeDtypeStruct((WIDE, right), jnp.float32),
            jax.ShapeDtypeStruct((rows, right), jnp.float32),
        ],
        scratch_shapes=[
            pltpu.VMEM((rows, WIDE), jnp.bfloat16),
            pltpu.VMEM((rows, WIDE), jnp.bfloat16),
            pltpu.VMEM((span, WIDE), jnp.bfloat16),
            pltpu.VMEM((span, WIDE), jnp.bfloat16),
        ],
        compiler_params=pltpu.CompilerParams(vmem_limit_bytes=56 * 1024 * 1024),
        name="update",
    )(inverse, wanted, columns, own, kernel, samples)


def on_device(kernel, row_block, panel_order, samples):
    rows_count = lax.axis_size("rows")
    cols_count = lax.axis_size("cols")
    cols_place = lax.axis_index("cols")
    blocks_here = row_block.shape[0]
    local_rows, local_cols = kernel.shape
    block_rows = local_rows // blocks_here
    per_panel = PW // block_rows
    share = blocks_here // cols_count
    right_cols = samples.shape[1]
    ranking = jnp.argsort(row_block)

    picked = []
    wanted = []
    for step in range(PANELS):
        start = panel_order[step] * PW
        owner = start // local_cols
        part = lax.dynamic_slice_in_dim(kernel, start - owner * local_cols, PW, 1)
        picked.append(jnp.where(cols_place == owner, part, jnp.zeros_like(part)))
        wanted.append(panel_order[step] * per_panel + jnp.arange(per_panel, dtype=jnp.int32))
    own = lax.psum(jnp.concatenate(picked, 1), "cols")

    own_blocks = own.reshape(blocks_here, block_rows, WIDE)
    wanted = jnp.concatenate(wanted, 0)
    matches = wanted[:, None] == row_block[None, :]
    held = jnp.any(matches, 1)[:, None, None]
    where = jnp.argmax(matches, 1)
    diag_part = jnp.where(held, jnp.take(own_blocks, where, axis=0), 0.0).reshape(WIDE, WIDE)
    right_part = jnp.where(
        held,
        jnp.take(samples.reshape(blocks_here, block_rows, right_cols), where, axis=0),
        0.0,
    ).reshape(WIDE, right_cols)
    diagonal, panel_right = lax.psum((diag_part, right_part), "rows")

    mine = lax.dynamic_slice_in_dim(ranking, cols_place * share, share, 0)
    piece = jnp.take(own_blocks, mine, axis=0)
    columns = (
        lax.all_gather(piece, "rows", axis=0)
        .transpose(1, 0, 2, 3)
        .reshape(local_cols, WIDE)
    )

    inverse = invert(diagonal)
    return tuple(update(inverse, panel_right, columns, own, kernel, samples))


def solution(mesh):
    in_specs = (P("rows", "cols"), P("rows"), P(), P("rows", "cols"))
    out_specs = (P("rows", "cols"), P("rows", None), P(None, "cols"), P("rows", "cols"))
    return jax.shard_map(
        on_device, mesh=mesh, in_specs=in_specs, out_specs=out_specs, check_vma=False
    )
```

time: 978 us -> 402 us (0.41)
  local copies, waits for them, and re-layouts: 337 us -> 19.6 us
  other arithmetic: 210 us -> 11 us
  Pallas kernels: 0 us -> 117 us
  matrix products: 93 us -> 0 us
  waiting for transfers between devices: 307 us -> 238 us
    transpose x3 -> x0, local copies, waits for them, and re-layouts: 131 us -> none  [on_device(): update = spread.reshape(local_rows, rows_count, share, block_rows).transp...]
    pallas_call x0 -> x2, Pallas kernels: none -> 117 us  [the longest x1 67.7 us: update(): pl.pallas_call(update_kernel, grid=(width // span, steps), in_specs=[pl.B...]
    reshape x4 -> x0, local copies, waits for them, and re-layouts: 111 us -> none  [the longest x2 109 us: on_device(): update = spread.reshape(local_rows, rows_count, share, block_rows).transp...]
    another operation x19 -> x1, other arithmetic: 109 us -> 0.7 us  [on_device(): where = jnp.argmax(matches, 1)]
    dot_general x12 -> x0, matrix products: 90.3 us -> none  [the longest x4 70.8 us: times_transposed(): lax.dot_general(left_side, right_side, (((1,), (1,)), ((), ())), precisio...]
    psum x2 -> x1, waiting for transfers between devices: 143 us -> 80.4 us  [on_device(): diagonal, panel_right = lax.psum((diag_part, right_part), 'rows')]
    gather x6 -> x3, local copies, waits for them, and re-layouts: 54.6 us -> 7.39 us  [the longest x1 2.8 us: on_device(): piece = jnp.take(own_blocks, mine, axis=0)]
    sub x1 -> x0, other arithmetic: 44 us -> none  [on_device(): trailing_work = trailing_work - update]
  transfers between devices with their start and end apart: 6 -> 3, of which waited for: 5 -> 3; matrix products, arithmetic and copies ran while one was open for 16% -> 2% of each run, Pallas kernels for 0% -> 12%
where the time goes in v1:
time: 402 us
  waiting for transfers between devices  238 us (59%)
  Pallas kernels  117 us (29%)
  local copies, waits for them, and re-layouts  19.6 us (5%)
  between operations  16.5 us (4%)
  other arithmetic  11 us (3%)
    psum x1, waiting for transfers between devices, on_device(): own = lax.psum(jnp.concatenate(picked, 1), 'cols')  81.3 us
    psum x1, waiting for transfers between devices, on_device(): diagonal, panel_right = lax.psum((diag_part, right_part), 'rows')  80.4 us
    all_gather x1, waiting for transfers between devices, on_device(): lax.all_gather(piece, 'rows', axis=0).transpose(1, 0, 2, 3)  76 us
    pallas_call x1, Pallas kernels, update(): pl.pallas_call(update_kernel, grid=(width // span, steps), in_specs=[pl.B...  67.7 us
    pallas_call x1, Pallas kernels, invert(): pl.pallas_call(invert_kernel, out_shape=jax.ShapeDtypeStruct((WIDE, WIDE)...  49 us
    all_gather x1, local copies, waits for them, and re-layouts, on_device(): lax.all_gather(piece, 'rows', axis=0).transpose(1, 0, 2, 3)  8.4 us
  transfers between devices with their start and end apart: 3, of which 3 were waited for; matrix products, arithmetic and copies ran while one was open for 2% of the time, Pallas kernels for 12%

profile of v1, /device:TPU:0, one launch (start us, length us, event | category | flops | bytes accessed | tf_op | source)
XLA Modules:
  0.0 401.7 jit_solution(13124319518010764413)
XLA Ops:
  7.2 0.0 all-reduce.4.cloned.1.call-start
  7.2 1.3 fusion.1
  9.9 2.5 dynamic-slice_select_fusion.1
  12.4 2.5 pad_maximum_fusion
  15.0 0.0 copy-start.2
  15.0 0.0 all-reduce.4.cloned.1.call-update
  15.0 0.0 all-reduce.6.cloned.1.call-start
  16.3 0.0 copy-done.2
  16.3 1.6 sort.17
  18.0 0.1 pad_add_fusion
  18.0 0.7 compare_reduce_fusion
  18.7 0.1 compare_and_fusion
  18.8 0.1 broadcast_in_dim.61
  18.9 0.1 broadcast_in_dim.62
  19.0 0.2 compare_reduce_fusion.1
  19.2 0.1 broadcast_in_dim.58
  19.2 0.1 broadcast_in_dim.59
  19.3 1.8 gather_fusion
  21.1 0.9 fusion
  22.0 81.3 %all-reduce.4.cloned.1.call-done.own_ref = f32[2048,512]{1,0:T(8,128)} async-done(((f32[2048,512]{1,0:T(8,128)}), f32[2048,512]{1,0:T(8,128)}) %all-reduce.4.cloned.1.call-update) | async-done | bytes 4194320 | tf_op jit(solution)/shard_map/psum | solution.py:223
  103.3 2.8 gather_fusion.1
  106.1 1.2 select_select_fusion
  107.3 0.0 all-reduce.6.cloned.1.call-update
  107.3 0.0 all-gather.3.cloned.1.call-start
  107.4 2.8 gather_fusion.2
  110.2 1.2 broadcast_select_fusion
  111.4 0.0 all-gather.3.cloned.1.call-update
  111.4 80.4 %all-reduce.6.cloned.1.call-done = (f32[512,512]{1,0:T(8,128)}, f32[512,128]{1,0:T(8,128)}) async-done(((f32[512,512]{1,0:T(8,128)}, f32[512,128]{1,0:T(8,128)}), (f32[512,512]{1,0:T(8,128)}, f32[512,128]{1,0:T(8,128)})) %all-reduce.6.cloned.1.call-update) | async-done | bytes 1310736 | tf_op jit(solution)/shard_map/psum | solution.py:236
  191.8 0.0 copy-start.1
  191.8 1.2 copy-done.1
  193.1 49.0 %invert.1.inverse_ref = f32[512,512]{1,0:T(8,128)S(1)} custom-call(f32[512,512]{1,0:T(8,128)S(1)} %copy-done.1), custom_call_target="tpu_custom_call" | custom-call | tf_op jit(solution)/shard_map/invert/pallas_call | solution.py:85
  242.1 0.0 copy-start
  242.1 1.0 copy-done
  243.1 76.0 %all-gather.3.cloned.1.call-done = f32[64,64,512]{2,1,0:T(8,128)} async-done(((f32[8,64,512]{2,1,0:T(8,128)}), f32[64,64,512]{2,1,0:T(8,128)}) %all-gather.3.cloned.1.call-update) | async-done | bytes 8388624 | tf_op jit(solution)/shard_map/all_gather | solution.py:241
  319.1 8.4 %copy.10 = f32[8,8,64,512]{3,2,0,1:T(8,128)} copy(f32[8,8,64,512]{3,2,1,0:T(8,128)} %bitcast.18) | data formatting | bytes 16777216 | tf_op jit(solution)/shard_map/all_gather | solution.py:241
  327.5 67.7 %update.1 = (f32[2048,4096]{1,0:T(8,128)}, f32[2048,512]{1,0:T(8,128)}, f32[512,128]{1,0:T(8,128)}, f32[2048,128]{1,0:T(8,128)}) custom-call(f32[512,512]{1,0:T(8,128)} %copy-done, f32[512,128]{1,0:T(8,128)} %get-tuple-element.10.wanted_ref, f32[4096,512]{1,0:T(8,128)} %bitcast.15, f32[2048,512]{1,0:T(8,128)} %all-reduce.4.cloned.1.call-done.own_ref, ...), custom_call_target="tpu_custom_call" | custom-call | tf_op jit(solution)/shard_map/update/pallas_call | solution.py:169
  (6 shorter events, 0.0 us)
Async XLA Ops:
  7.2 96.1 %all-reduce.4.cloned.1.call-start = ((), (), s32[]{:S(2)}) async-start(), calls=%async_computation | async-start | bytes 8388608 | tf_op jit(solution)/shard_map/psum | solution.py:223
  15.0 1.4 copy-start.2
  15.0 176.9 %all-reduce.6.cloned.1.call-start = ((), (), s32[]{:S(2)}) async-start(), calls=%async_computation.2 | async-start | bytes 2621440 | tf_op jit(solution)/shard_map/psum | solution.py:236
  107.3 211.8 %all-gather.3.cloned.1.call-start = ((), (), s32[]{:S(2)}) async-start(), calls=%async_computation.1 | async-start | bytes 9437184 | tf_op jit(solution)/shard_map/all_gather | solution.py:241
  191.8 1.2 copy-start.1
  242.1 1.0 copy-start
Sparse Core Ops, SparseCore 0:
  15.1 88.1 all-reduce.3
  107.9 83.8 all-reduce.5
  194.6 124.4 all-gather.2

commit v2 on v1

--- a/solution.py
+++ b/solution.py
@@ -17,40 +17,26 @@
 
 
 def eliminate(block):
-    strips = [block[s * STRIP : (s + 1) * STRIP, :] for s in range(SUB // STRIP)]
-    row_id = lax.broadcasted_iota(jnp.int32, (STRIP, SUB), 0)
-    lane_id = lax.broadcasted_iota(jnp.int32, (STRIP, SUB), 1)
-    right = [
-        jnp.where(lane_id == row_id + s * STRIP, 1.0, 0.0).astype(jnp.float32)
-        for s in range(SUB // STRIP)
-    ]
-    below = lax.broadcasted_iota(jnp.int32, (STRIP, 1), 0)
-    pivots = [jnp.zeros((STRIP, 1), jnp.float32) for s in range(SUB // STRIP)]
+    rows = lax.broadcasted_iota(jnp.int32, (SUB, SUB), 0)
+    lanes = lax.broadcasted_iota(jnp.int32, (SUB, SUB), 1)
+    place = lax.broadcasted_iota(jnp.int32, (SUB, 1), 0)
+    left = block
+    right = jnp.where(rows == lanes, 1.0, 0.0).astype(jnp.float32)
+    pivots = jnp.ones((SUB, 1), jnp.float32)
     for col in range(SUB):
-        home, place = divmod(col, STRIP)
-        row_left = strips[home][place : place + 1, :]
-        row_right = right[home][place : place + 1, :]
+        row_left = left[col : col + 1, :]
         pivot = row_left[:, col : col + 1]
         scale = 1.0 / pivot
-        pivots[home] = jnp.where(below == place, pivot, pivots[home])
-        scaled_left = row_left * scale
-        scaled_right = row_right * scale
-        for s in range(home, SUB // STRIP):
-            if s == home and place == STRIP - 1:
-                continue
-            ratio = strips[s][:, col : col + 1]
-            if s == home:
-                ratio = jnp.where(below > place, ratio, 0.0)
-            strips[s] = strips[s] - ratio * scaled_left
-            right[s] = right[s] - ratio * scaled_right
-    return jnp.concatenate(
-        [right[s] * lax.rsqrt(pivots[s]) for s in range(SUB // STRIP)], axis=0
-    )
-
-
-def invert_kernel(diag_ref, out_ref, work):
+        pivots = jnp.where(place == col, pivot, pivots)
+        ratio = jnp.where(place > col, left[:, col : col + 1], 0.0)
+        row_right = right[col : col + 1, :] * scale
+        left = left - ratio * (row_left * scale)
+        right = right - ratio * row_right
+    return right * lax.rsqrt(pivots)
+
+
+def invert_steps(work, between):
     count = WIDE // SUB
-    work[:, :WIDE] = diag_ref[...]
     rows = lax.broadcasted_iota(jnp.int32, (WIDE, WIDE), 0)
     lanes = lax.broadcasted_iota(jnp.int32, (WIDE, WIDE), 1)
     work[:, WIDE:] = jnp.where(rows == lanes, 1.0, 0.0).astype(jnp.float32)
@@ -58,26 +44,31 @@
     def step(k, carry):
         here = pl.ds(pl.multiple_of(k * SUB, SUB), SUB)
         inverse = eliminate(work[here, here])
-        scaled = jnp.dot(
+        between(k, 0)
+        work[here, :] = jnp.dot(
             inverse, work[here, :], precision=EXACT, preferred_element_type=jnp.float32
         )
-        work[here, :] = scaled
         for i in range(1, count):
 
             @pl.when(i > k)
             def _():
-                left = work[here, i * SUB : (i + 1) * SUB]
                 work[i * SUB : (i + 1) * SUB, :] -= lax.dot_general(
-                    left,
+                    work[here, i * SUB : (i + 1) * SUB],
                     work[here, :],
                     (((0,), (0,)), ((), ())),
                     precision=EXACT,
                     preferred_element_type=jnp.float32,
                 )
 
+        between(k, 1)
         return carry
 
     lax.fori_loop(0, count, step, 0)
+
+
+def invert_kernel(diag_ref, out_ref, work):
+    work[:, :WIDE] = diag_ref[...]
+    invert_steps(work, lambda k, turn: None)
     out_ref[...] = work[:, WIDE:]
 
 
@@ -93,6 +84,184 @@
     )(diagonal)
 
 
+def ring_index(position):
+    turn = position // 4
+    return 2 * (position + turn * (7 - 2 * position)) + turn
+
+
+def exchange_kernel(
+    parts_ref, diag_ref, right_ref,
+    own_ref, columns_ref, wanted_ref, out_ref,
+    parts_in, diag_in, diag_all, right_all, slabs, work,
+    part_sem, diag_sem, row_sem, right_sem, slab_sem, own_sem, ring_sem,
+):
+    i = lax.axis_index("rows")
+    j = lax.axis_index("cols")
+    place = (i // 2) + (i % 2) * (7 - 2 * (i // 2))
+    after = ring_index((place + 1) % 8)
+    before = ring_index((place + 7) % 8)
+    half = columns_ref.shape[1] // 2
+    rights = right_ref.shape[1]
+    block_rows = SUB // PANELS
+
+    def to(src, dst, sems, row, col):
+        return pltpu.make_async_remote_copy(
+            src_ref=src, dst_ref=dst, send_sem=sems.at[0], recv_sem=sems.at[1],
+            device_id=(row, col), device_id_type=pl.DeviceIdType.MESH,
+        )
+
+    barrier = pltpu.get_barrier_semaphore()
+    for d in range(1, 4):
+        pl.semaphore_signal(
+            barrier, inc=1, device_id=(i, (j + d) % 4), device_id_type=pl.DeviceIdType.MESH
+        )
+    for d in range(1, 8):
+        pl.semaphore_signal(
+            barrier, inc=1, device_id=((i + d) % 8, j), device_id_type=pl.DeviceIdType.MESH
+        )
+    pl.semaphore_wait(barrier, 10)
+
+    sent = []
+    diag_copies = []
+    part_copies = []
+    right_copies = []
+    for d in range(1, 4):
+        there = (j + d) % 4
+        diag_copies.append(to(diag_ref.at[there], diag_in.at[d - 1], diag_sem.at[d - 1], i, there))
+        diag_copies[-1].start()
+    for d in range(1, 4):
+        there = (j + d) % 4
+        part_copies.append(to(parts_ref.at[there], parts_in.at[d - 1], part_sem.at[d - 1], i, there))
+        part_copies[-1].start()
+    right_all[i] = right_ref[...]
+    for d in range(1, 8):
+        right_copies.append(
+            to(right_all.at[i], right_all.at[i], right_sem.at[d - 1], (i + d) % 8, j)
+        )
+        right_copies[-1].start()
+
+    total = diag_ref[j]
+    for d in range(3):
+        diag_copies[d].wait()
+        total = total + diag_in[d]
+    diag_all[i] = total
+    row_copies = []
+    for d in range(1, 8):
+        row_copies.append(to(diag_all.at[i], diag_all.at[i], row_sem.at[d - 1], (i + d) % 8, j))
+        row_copies[-1].start()
+
+    for d in range(3):
+        part_copies[d].wait()
+    piece = parts_ref[j] + parts_in[0] + parts_in[1] + parts_in[2]
+    columns_ref[i] = piece
+    own_ref[j] = piece
+
+    def ring_copy(step, way):
+        origin = ring_index((place + (8 - step if way == 0 else step)) % 8)
+        target = after if way == 0 else before
+        spot = columns_ref.at[origin, pl.ds(way * half, half)]
+        return to(spot, spot, ring_sem.at[way, step], target, j)
+
+    def ring_arrival(step, way):
+        origin = ring_index((place + (7 - step if way == 0 else step + 1)) % 8)
+        spot = columns_ref.at[origin, pl.ds(way * half, half)]
+        return to(spot, spot, ring_sem.at[way, step], after if way == 0 else before, j)
+
+    def ring_step(step):
+        for way in range(2):
+            ring_arrival(step - 1, way).wait_recv()
+            ring_copy(step, way).start()
+
+    for way in range(2):
+        ring_copy(0, way).start()
+    own_copies = []
+    for d in range(1, 4):
+        own_copies.append(to(own_ref.at[j], own_ref.at[j], own_sem.at[d - 1], i, (j + d) % 4))
+        own_copies[-1].start()
+
+    def arrival(buffer, sems, d):
+        here = (i + 8 - d) % 8
+        return to(buffer.at[here], buffer.at[here], sems.at[d - 1], here, j)
+
+    for d in range(1, 8):
+        arrival(diag_all, row_sem, d).wait_recv()
+    for q in range(4):
+        both = diag_all[q] + diag_all[q + 4]
+        for panel in range(PANELS):
+            slabs[j, panel * PW + q * block_rows : panel * PW + (q + 1) * block_rows, :] = both[
+                panel * block_rows : (panel + 1) * block_rows, :
+            ]
+    slab_copies = []
+    for d in range(1, 4):
+        slab_copies.append(to(slabs.at[j], slabs.at[j], slab_sem.at[d - 1], i, (j + d) % 4))
+        slab_copies[-1].start()
+    ring_step(1)
+    for d in range(1, 8):
+        arrival(right_all, right_sem, d).wait_recv()
+    for q in range(4):
+        both = right_all[q] + right_all[q + 4]
+        for panel in range(PANELS):
+            wanted_ref[panel * PW + q * block_rows : panel * PW + (q + 1) * block_rows, :] = both[
+                panel * block_rows : (panel + 1) * block_rows, :
+            ]
+    for d in range(1, 4):
+        here = (j + 4 - d) % 4
+        to(slabs.at[here], slabs.at[here], slab_sem.at[d - 1], i, here).wait_recv()
+    for q in range(4):
+        work[:, q * SUB : (q + 1) * SUB] = slabs[q]
+    ring_step(2)
+
+    def between(k, turn):
+        @pl.when(k < 2)
+        def _():
+            ring_step(3 + 2 * k + turn)
+
+    invert_steps(work, between)
+    out_ref[...] = work[:, WIDE:]
+
+    for way in range(2):
+        ring_arrival(6, way).wait_recv()
+        for step in range(7):
+            ring_copy(step, way).wait_send()
+    for d in range(1, 4):
+        here = (j + 4 - d) % 4
+        to(own_ref.at[here], own_ref.at[here], own_sem.at[d - 1], i, here).wait_recv()
+    for copy in own_copies + slab_copies + row_copies + right_copies:
+        copy.wait_send()
+
+
+def exchange(parts, diag, right):
+    share = parts.shape[1]
+    rights = right.shape[1]
+    whole = pl.BlockSpec(memory_space=pltpu.VMEM)
+    sems = pltpu.SemaphoreType.DMA
+    return pl.pallas_call(
+        exchange_kernel,
+        in_specs=[whole] * 3,
+        out_specs=[whole] * 4,
+        out_shape=[
+            jax.ShapeDtypeStruct(parts.shape, jnp.float32),
+            jax.ShapeDtypeStruct((8, share, WIDE), jnp.float32),
+            jax.ShapeDtypeStruct((WIDE, rights), jnp.float32),
+            jax.ShapeDtypeStruct((WIDE, WIDE), jnp.float32),
+        ],
+        scratch_shapes=[
+            pltpu.VMEM((3, share, WIDE), jnp.float32),
+            pltpu.VMEM((3, SUB, SUB), jnp.float32),
+            pltpu.VMEM((8, SUB, SUB), jnp.float32),
+            pltpu.VMEM((8, SUB, rights), jnp.float32),
+            pltpu.VMEM((4, WIDE, SUB), jnp.float32),
+            pltpu.VMEM((WIDE, 2 * WIDE), jnp.float32),
+            sems((3, 2)), sems((3, 2)), sems((7, 2)), sems((7, 2)), sems((3, 2)), sems((3, 2)),
+            sems((2, 7, 2)),
+        ],
+        compiler_params=pltpu.CompilerParams(
+            collective_id=0, has_side_effects=True, vmem_limit_bytes=48 * 1024 * 1024
+        ),
+        name="exchange",
+    )(parts, diag, right)
+
+
 def halves(value):
     high = value.astype(jnp.bfloat16)
     low = (value - high.astype(jnp.float32)).astype(jnp.bfloat16)
@@ -136,7 +305,8 @@
 
     @pl.when(i == 0)
     def _():
-        high, low = halves(times_transposed(cols_ref[...], inverse_ref[...]))
+        columns = cols_ref[...].swapaxes(0, 1).reshape(cols_high.shape)
+        high, low = halves(times_transposed(columns, inverse_ref[...]))
         cols_high[...] = high
         cols_low[...] = low
 
@@ -162,6 +332,8 @@
     tile = min(512, rows)
     span = min(1024, width)
     steps = rows // tile
+    groups, _, block_rows, _ = columns.shape
+    runs = span // (groups * block_rows)
 
     def first(j, i):
         return (jnp.where(j == 0, i, steps - 1), 0)
@@ -172,7 +344,7 @@
         in_specs=[
             pl.BlockSpec((WIDE, WIDE), lambda j, i: (0, 0)),
             pl.BlockSpec((WIDE, right), lambda j, i: (0, 0)),
-            pl.BlockSpec((span, WIDE), lambda j, i: (j, 0)),
+            pl.BlockSpec((groups, runs, block_rows, WIDE), lambda j, i: (0, j, 0, 0)),
             pl.BlockSpec((tile, WIDE), first),
             pl.BlockSpec((tile, span), lambda j, i: (i, j)),
             pl.BlockSpec((tile, right), first),
@@ -220,30 +392,37 @@
         part = lax.dynamic_slice_in_dim(kernel, start - owner * local_cols, PW, 1)
         picked.append(jnp.where(cols_place == owner, part, jnp.zeros_like(part)))
         wanted.append(panel_order[step] * per_panel + jnp.arange(per_panel, dtype=jnp.int32))
-    own = lax.psum(jnp.concatenate(picked, 1), "cols")
-
-    own_blocks = own.reshape(blocks_here, block_rows, WIDE)
-    wanted = jnp.concatenate(wanted, 0)
-    matches = wanted[:, None] == row_block[None, :]
-    held = jnp.any(matches, 1)[:, None, None]
-    where = jnp.argmax(matches, 1)
-    diag_part = jnp.where(held, jnp.take(own_blocks, where, axis=0), 0.0).reshape(WIDE, WIDE)
-    right_part = jnp.where(
-        held,
-        jnp.take(samples.reshape(blocks_here, block_rows, right_cols), where, axis=0),
-        0.0,
-    ).reshape(WIDE, right_cols)
-    diagonal, panel_right = lax.psum((diag_part, right_part), "rows")
-
-    mine = lax.dynamic_slice_in_dim(ranking, cols_place * share, share, 0)
-    piece = jnp.take(own_blocks, mine, axis=0)
-    columns = (
-        lax.all_gather(piece, "rows", axis=0)
-        .transpose(1, 0, 2, 3)
-        .reshape(local_cols, WIDE)
-    )
-
-    inverse = invert(diagonal)
+    picked = jnp.concatenate(picked, 1).reshape(blocks_here, block_rows, WIDE)
+    sample_blocks = samples.reshape(blocks_here, block_rows, right_cols)
+
+    def held_rows(blocks, names):
+        matches = names[:, None] == row_block[None, :]
+        held = jnp.any(matches, 1)[:, None, None]
+        found = jnp.where(held, jnp.take(blocks, jnp.argmax(matches, 1), axis=0), 0.0)
+        return found.reshape(-1, blocks.shape[2])
+
+    if (rows_count, cols_count) == (8, 4) and per_panel == 4:
+        place = lax.axis_index("rows") % per_panel
+        names = jnp.stack([panel_order[step] * per_panel + place for step in range(PANELS)])
+        parts = jnp.take(picked, ranking, axis=0).reshape(cols_count, share * block_rows, WIDE)
+        diag = held_rows(picked, names).reshape(-1, cols_count, SUB).transpose(1, 0, 2)
+        right = held_rows(sample_blocks, names)
+        own, columns, panel_right, inverse = exchange(parts, diag, right)
+        own = jnp.take(
+            own.reshape(blocks_here, block_rows, WIDE), row_block // rows_count, axis=0
+        ).reshape(local_rows, WIDE)
+        columns = columns.reshape(rows_count, share, block_rows, WIDE)
+    else:
+        names = jnp.concatenate(wanted, 0)
+        own_blocks = lax.psum(picked, "cols")
+        own = own_blocks.reshape(local_rows, WIDE)
+        diagonal, panel_right = lax.psum(
+            (held_rows(own_blocks, names), held_rows(sample_blocks, names)), "rows"
+        )
+        mine = lax.dynamic_slice_in_dim(ranking, cols_place * share, share, 0)
+        columns = lax.all_gather(jnp.take(own_blocks, mine, axis=0), "rows", axis=0)
+        columns = columns.transpose(1, 0, 2, 3).reshape(1, -1, block_rows, WIDE)
+        inverse = invert(diagonal)
     return tuple(update(inverse, panel_right, columns, own, kernel, samples))
 
 

time: 402 us -> 297 us (0.74); the launches traced: 402 us -> 291 us
  waiting for transfers between devices: 238 us -> 0 us
  Pallas kernels: 117 us -> 247 us
  between operations: 16.5 us -> 3.54 us
  other arithmetic: 11 us -> 20.5 us
    psum x2 -> x0, waiting for transfers between devices: 162 us -> none  [the longest x1 81.3 us: on_device(): own = lax.psum(jnp.concatenate(picked, 1), 'cols')]
    pallas_call x1, Pallas kernels: 49 us -> 180 us  [exchange(): pl.pallas_call(exchange_kernel, in_specs=[whole] * 3, out_specs=[whole] *...]
    all_gather x1 -> x0, waiting for transfers between devices: 76 us -> none  [on_device(): lax.all_gather(piece, 'rows', axis=0).transpose(1, 0, 2, 3)]
    all_gather x1 -> x0, local copies, waits for them, and re-layouts: 8.4 us -> none  [on_device(): lax.all_gather(piece, 'rows', axis=0).transpose(1, 0, 2, 3)]
    gather x3 -> x5, local copies, waits for them, and re-layouts: 7.39 us -> 14.6 us  [the longest x1 5.02 us: on_device(): jnp.take(picked, ranking, axis=0)]
    select_n x4 -> x5, other arithmetic: 3.29 us -> 10.1 us  [the longest x2 5.03 us: on_device(): jnp.take(picked, ranking, axis=0)]
  transfers between devices with their start and end apart: 3 -> 0, of which waited for: 3 -> 0; matrix products, arithmetic and copies ran while one was open for 2% -> 0% of each run, Pallas kernels for 12% -> 0%
where the time goes in v2:
time: 297 us; the launch traced here: 291 us
  Pallas kernels  247 us (83%)
  other arithmetic  20.5 us (7%)
  local copies, waits for them, and re-layouts  20 us (7%)
  between operations  3.54 us (1%)
    pallas_call x1, Pallas kernels, exchange(): pl.pallas_call(exchange_kernel, in_specs=[whole] * 3, out_specs=[whole] *...  180 us
    pallas_call x1, Pallas kernels, update(): pl.pallas_call(update_kernel, grid=(width // span, steps), in_specs=[pl.B...  67.4 us

profile of v2, /device:TPU:0, one launch (start us, length us, event | category | flops | bytes accessed | tf_op | source)
XLA Modules:
  0.0 291.5 jit_solution(17770123386455569800)
XLA Ops:
  0.7 2.3 sort.17
  2.9 0.7 compare_and_fusion
  3.6 1.3 fusion.3
  7.6 0.1 pad_add_fusion
  7.6 0.8 compare_reduce_fusion.1
  8.5 0.1 broadcast_in_dim.69
  8.5 0.1 broadcast_in_dim.70
  8.6 1.4 compare_reduce_fusion
  10.0 0.1 broadcast_in_dim.72
  10.1 0.1 broadcast_in_dim.73
  10.2 1.8 gather_fusion.1
  12.0 0.1 fusion.2.right_ref
  12.1 2.5 dynamic-slice_select_fusion.1
  14.6 2.5 pad_maximum_fusion
  17.1 2.7 gather_fusion
  19.9 5.0 %gather_fusion.2 = f32[32,64,512]{2,1,0:T(8,128)} fusion(f32[32,64,512]{2,1,0:T(8,128)} %bitcast.20, s32[1024]{0:T(1024)S(1)} %pad_clamp_fusion.2), kind=kCustom, calls=%fused_computation.clone | custom fusion | bytes 8388736 | tf_op jit(solution)/shard_map/jit(_take)/gather | solution.py:407
  24.9 5.0 %broadcast_select_fusion.1 = f32[32,64,512]{2,1,0:T(8,128)} fusion(f32[32,64,512]{2,1,0:T(8,128)} %gather_fusion.2, pred[32]{0:T(512)(128)(4,1)S(1)} %get-tuple-element.23), kind=kLoop, calls=%fused_computation.6 | loop fusion | flops 1048576 | bytes 8388640 | tf_op jit(solution)/shard_map/jit(_take)/select_n | solution.py:407
  29.9 0.1 gather.16
  30.0 0.1 fusion.1.diag_ref
  30.2 180.0 %exchange.1 = (f32[4,512,512]{2,1,0:T(8,128)S(1)}, f32[8,512,512]{2,1,0:T(8,128)}, f32[512,128]{1,0:T(8,128)S(1)}, f32[512,512]{1,0:T(8,128)S(1)}) custom-call(f32[4,512,512]{2,1,0:T(8,128)} %bitcast.22, f32[4,128,128]{2,1,0:T(8,128)S(1)} %fusion.1.diag_ref, f32[128,128]{1,0:T(8,128)S(1)} %fusion.2.right_ref), custom_call_target="tpu_custom_call" | custom-call | tf_op jit(solution)/shard_map/exchange/pallas_call | solution.py:238
  210.2 0.0 copy-start
  210.2 2.0 copy-done
  212.2 0.0 copy-start.1
  212.2 1.0 copy-done.1
  213.2 0.0 copy-start.2
  213.2 0.7 copy-done.2
  213.9 5.0 %gather_fusion.3 = f32[32,64,512]{2,1,0:T(8,128)} fusion(f32[32,64,512]{2,1,0:T(8,128)} %bitcast.18, s32[1024]{0:T(1024)S(1)} %pad_clamp_fusion), kind=kCustom, calls=%fused_computation.1.clone | custom fusion | bytes 8388736 | tf_op jit(solution)/shard_map/jit(_take)/gather | solution.py:411
  218.9 5.0 %broadcast_select_fusion = f32[32,64,512]{2,1,0:T(8,128)} fusion(f32[32,64,512]{2,1,0:T(8,128)} %gather_fusion.3, pred[32]{0:T(512)(128)(4,1)S(1)} %get-tuple-element.17), kind=kLoop, calls=%fused_computation.5 | loop fusion | flops 1048576 | bytes 8388640 | tf_op jit(solution)/shard_map/jit(_take)/select_n | solution.py:411
  223.9 67.4 %update.1 = (f32[2048,4096]{1,0:T(8,128)}, f32[2048,512]{1,0:T(8,128)}, f32[512,128]{1,0:T(8,128)}, f32[2048,128]{1,0:T(8,128)}) custom-call(f32[512,512]{1,0:T(8,128)} %copy-done.1, f32[512,128]{1,0:T(8,128)} %copy-done.2, f32[8,8,64,512]{3,2,1,0:T(8,128)} %bitcast.23, f32[2048,512]{1,0:T(8,128)} %bitcast.21, f32[2048,4096]{1,0:T(8,128)} %kernel_ref.1, ...), custom_call_target="tpu_custom_call" | custom-call | tf_op jit(solution)/shard_map/update/pallas_call | solution.py:341
  (7 shorter events, 0.0 us)
Async XLA Ops:
  210.2 2.0 copy-start
  212.2 1.1 copy-start.1
  213.2 0.7 copy-start.2

commit v3 on v2

--- a/solution.py
+++ b/solution.py
@@ -11,28 +11,31 @@
 PANELS = 2
 WIDE = PW * PANELS
 SUB = 128
-STRIP = 8
+STRIP = 16
 
 EXACT = lax.Precision.HIGHEST
 
 
 def eliminate(block):
+    strips = [block[s * STRIP : (s + 1) * STRIP, :] for s in range(SUB // STRIP)]
+    place = lax.broadcasted_iota(jnp.int32, (STRIP, 1), 0)
+    lane = lax.broadcasted_iota(jnp.int32, (1, SUB), 1)
+    for col in range(SUB):
+        home, spot = divmod(col, STRIP)
+        row = strips[home][spot : spot + 1, :]
+        scale = 1.0 / row[:, col : col + 1]
+        scaled = jnp.where(lane == col, 1.0 + scale, row * scale)
+        for s in range(home, SUB // STRIP):
+            ratio = strips[s][:, col : col + 1]
+            if s == home:
+                ratio = jnp.where(place > spot, ratio, 0.0)
+            strips[s] = strips[s] - ratio * scaled
+    merged = jnp.concatenate(strips, axis=0)
     rows = lax.broadcasted_iota(jnp.int32, (SUB, SUB), 0)
     lanes = lax.broadcasted_iota(jnp.int32, (SUB, SUB), 1)
-    place = lax.broadcasted_iota(jnp.int32, (SUB, 1), 0)
-    left = block
-    right = jnp.where(rows == lanes, 1.0, 0.0).astype(jnp.float32)
-    pivots = jnp.ones((SUB, 1), jnp.float32)
-    for col in range(SUB):
-        row_left = left[col : col + 1, :]
-        pivot = row_left[:, col : col + 1]
-        scale = 1.0 / pivot
-        pivots = jnp.where(place == col, pivot, pivots)
-        ratio = jnp.where(place > col, left[:, col : col + 1], 0.0)
-        row_right = right[col : col + 1, :] * scale
-        left = left - ratio * (row_left * scale)
-        right = right - ratio * row_right
-    return right * lax.rsqrt(pivots)
+    pivots = jnp.sum(jnp.where(rows == lanes, merged, 0.0), axis=1, keepdims=True)
+    lower = jnp.where(rows > lanes, merged, jnp.where(rows == lanes, 1.0, 0.0))
+    return lower * lax.rsqrt(pivots)
 
 
 def invert_steps(work, between):
@@ -44,7 +47,7 @@
     def step(k, carry):
         here = pl.ds(pl.multiple_of(k * SUB, SUB), SUB)
         inverse = eliminate(work[here, here])
-        between(k, 0)
+        between(k)
         work[here, :] = jnp.dot(
             inverse, work[here, :], precision=EXACT, preferred_element_type=jnp.float32
         )
@@ -60,7 +63,6 @@
                     preferred_element_type=jnp.float32,
                 )
 
-        between(k, 1)
         return carry
 
     lax.fori_loop(0, count, step, 0)
@@ -68,7 +70,7 @@
 
 def invert_kernel(diag_ref, out_ref, work):
     work[:, :WIDE] = diag_ref[...]
-    invert_steps(work, lambda k, turn: None)
+    invert_steps(work, lambda k: None)
     out_ref[...] = work[:, WIDE:]
 
 
@@ -211,12 +213,7 @@
         work[:, q * SUB : (q + 1) * SUB] = slabs[q]
     ring_step(2)
 
-    def between(k, turn):
-        @pl.when(k < 2)
-        def _():
-            ring_step(3 + 2 * k + turn)
-
-    invert_steps(work, between)
+    invert_steps(work, lambda k: ring_step(3 + k))
     out_ref[...] = work[:, WIDE:]
 
     for way in range(2):
@@ -278,19 +275,10 @@
     )
 
 
-def split_product(left, right):
-    def one(a, b):
-        return lax.dot_general(
-            a, b, (((1,), (1,)), ((), ())), preferred_element_type=jnp.float32
-        )
-
-    return one(left[0], right[0]) + (one(left[0], right[1]) + one(left[1], right[0]))
-
-
 def update_kernel(
     inverse_ref, wanted_ref, cols_ref, own_ref, kernel_ref, samples_ref,
     trailing_ref, factor_ref, solved_ref, reduced_ref,
-    own_high, own_low, cols_high, cols_low,
+    own_halves, cols_halves,
 ):
     j = pl.program_id(0)
     i = pl.program_id(1)
@@ -305,24 +293,26 @@
 
     @pl.when(i == 0)
     def _():
-        columns = cols_ref[...].swapaxes(0, 1).reshape(cols_high.shape)
-        high, low = halves(times_transposed(columns, inverse_ref[...]))
-        cols_high[...] = high
-        cols_low[...] = low
+        columns = cols_ref[...].swapaxes(0, 1).reshape(-1, WIDE)
+        high, low = halves(times_transposed(inverse_ref[...], columns))
+        cols_halves[:WIDE, :] = high
+        cols_halves[WIDE : 2 * WIDE, :] = low
+        cols_halves[2 * WIDE :, :] = high
 
     @pl.when(j == 0)
     def _():
         factor = times_transposed(own_ref[...], inverse_ref[...])
         factor_ref[...] = factor
         high, low = halves(factor)
-        own_high[at, :] = high
-        own_low[at, :] = low
+        own_halves[at, :WIDE] = high
+        own_halves[at, WIDE : 2 * WIDE] = high
+        own_halves[at, 2 * WIDE :] = low
         reduced_ref[...] = samples_ref[...] - jnp.dot(
             factor, solved_ref[...], precision=EXACT, preferred_element_type=jnp.float32
         )
 
-    trailing_ref[...] = kernel_ref[...] - split_product(
-        (own_high[at, :], own_low[at, :]), (cols_high[...], cols_low[...])
+    trailing_ref[...] = kernel_ref[...] - jnp.dot(
+        own_halves[at, :], cols_halves[...], preferred_element_type=jnp.float32
     )
 
 
@@ -362,10 +352,8 @@
             jax.ShapeDtypeStruct((rows, right), jnp.float32),
         ],
         scratch_shapes=[
-            pltpu.VMEM((rows, WIDE), jnp.bfloat16),
-            pltpu.VMEM((rows, WIDE), jnp.bfloat16),
-            pltpu.VMEM((span, WIDE), jnp.bfloat16),
-            pltpu.VMEM((span, WIDE), jnp.bfloat16),
+            pltpu.VMEM((rows, 3 * WIDE), jnp.bfloat16),
+            pltpu.VMEM((3 * WIDE, span), jnp.bfloat16),
         ],
         compiler_params=pltpu.CompilerParams(vmem_limit_bytes=56 * 1024 * 1024),
         name="update",
@@ -382,7 +370,9 @@
     per_panel = PW // block_rows
     share = blocks_here // cols_count
     right_cols = samples.shape[1]
-    ranking = jnp.argsort(row_block)
+    ranking = jnp.argmax(
+        (row_block // rows_count)[None, :] == jnp.arange(blocks_here, dtype=jnp.int32)[:, None], 1
+    )
 
     picked = []
     wanted = []
@@ -398,18 +388,18 @@
     def held_rows(blocks, names):
         matches = names[:, None] == row_block[None, :]
         held = jnp.any(matches, 1)[:, None, None]
-        found = jnp.where(held, jnp.take(blocks, jnp.argmax(matches, 1), axis=0), 0.0)
+        found = jnp.where(held, jnp.take(blocks, jnp.argmax(matches, 1), axis=0, mode="clip"), 0.0)
         return found.reshape(-1, blocks.shape[2])
 
     if (rows_count, cols_count) == (8, 4) and per_panel == 4:
         place = lax.axis_index("rows") % per_panel
         names = jnp.stack([panel_order[step] * per_panel + place for step in range(PANELS)])
-        parts = jnp.take(picked, ranking, axis=0).reshape(cols_count, share * block_rows, WIDE)
+        parts = jnp.take(picked, ranking, axis=0, mode="clip").reshape(cols_count, share * block_rows, WIDE)
         diag = held_rows(picked, names).reshape(-1, cols_count, SUB).transpose(1, 0, 2)
         right = held_rows(sample_blocks, names)
         own, columns, panel_right, inverse = exchange(parts, diag, right)
         own = jnp.take(
-            own.reshape(blocks_here, block_rows, WIDE), row_block // rows_count, axis=0
+            own.reshape(blocks_here, block_rows, WIDE), row_block // rows_count, axis=0, mode="clip"
         ).reshape(local_rows, WIDE)
         columns = columns.reshape(rows_count, share, block_rows, WIDE)
     else:
@@ -420,7 +410,7 @@
             (held_rows(own_blocks, names), held_rows(sample_blocks, names)), "rows"
         )
         mine = lax.dynamic_slice_in_dim(ranking, cols_place * share, share, 0)
-        columns = lax.all_gather(jnp.take(own_blocks, mine, axis=0), "rows", axis=0)
+        columns = lax.all_gather(jnp.take(own_blocks, mine, axis=0, mode="clip"), "rows", axis=0)
         columns = columns.transpose(1, 0, 2, 3).reshape(1, -1, block_rows, WIDE)
         inverse = invert(diagonal)
     return tuple(update(inverse, panel_right, columns, own, kernel, samples))

time: 297 us -> 276 us (0.929)
  other arithmetic: 20.5 us -> 8.81 us
  Pallas kernels: 247 us -> 239 us
    select_n x5 -> x2, other arithmetic: 10.1 us -> 0.75 us  [the longest x1 0.67 us: on_device(): row_block // rows_count]
    pallas_call x1, Pallas kernels: 180 us -> 172 us  [exchange(): pl.pallas_call(exchange_kernel, in_specs=[whole] * 3, out_specs=[whole] *...]
where the time goes in v3:
time: 276 us; the launch traced here: 271 us
  Pallas kernels  239 us (87%)
  local copies, waits for them, and re-layouts  19.8 us (7%)
  other arithmetic  8.81 us (3%)
  between operations  3.53 us (1%)
    pallas_call x1, Pallas kernels, exchange(): pl.pallas_call(exchange_kernel, in_specs=[whole] * 3, out_specs=[whole] *...  172 us
    pallas_call x1, Pallas kernels, update(): pl.pallas_call(update_kernel, grid=(width // span, steps), in_specs=[pl.B...  67.3 us

profile of v3, /device:TPU:0, one launch (start us, length us, event | category | flops | bytes accessed | tf_op | source)
XLA Modules:
  0.0 271.0 jit_solution(4357894739941828966)
XLA Ops:
  0.6 0.7 and_select_fusion
  1.3 1.3 fusion.1
  5.3 0.1 pad_add_fusion
  5.4 0.8 compare_reduce_fusion.1
  6.2 0.1 broadcast_in_dim.50
  6.3 0.1 broadcast_in_dim.51
  6.4 1.4 compare_reduce_fusion
  7.7 0.6 iota_reduce_fusion
  8.4 1.8 gather_fusion.2
  10.2 0.1 bitcast_select_fusion.right_ref
  10.2 2.5 dynamic-slice_select_fusion.1
  12.8 2.5 pad_maximum_fusion
  15.3 2.7 %gather_fusion.1 = f32[2,64,512]{2,1,0:T(8,128)S(1)} fusion(f32[32,64,512]{2,1,0:T(8,128)} %bitcast.17, s32[1024]{0:T(1024)S(1)} %pad_clamp_fusion.1), kind=kCustom, calls=%fused_computation.1 | custom fusion | bytes 524296 | tf_op jit(solution)/shard_map/jit(_take)/gather | solution.py:391
  18.1 5.0 %gather_fusion = f32[32,64,512]{2,1,0:T(8,128)} fusion(f32[32,64,512]{2,1,0:T(8,128)} %bitcast.18, s32[1024]{0:T(1024)S(1)} %pad_clamp_fusion.2), kind=kCustom, calls=%fused_computation | custom fusion | bytes 8388736 | tf_op jit(solution)/shard_map/jit(_take)/gather | solution.py:397
  23.1 0.1 gather.21
  23.2 0.1 fusion.diag_ref
  23.3 171.5 %exchange.1 = (f32[4,512,512]{2,1,0:T(8,128)S(1)}, f32[8,512,512]{2,1,0:T(8,128)}, f32[512,128]{1,0:T(8,128)S(1)}, f32[512,512]{1,0:T(8,128)S(1)}) custom-call(f32[4,512,512]{2,1,0:T(8,128)} %bitcast.20, f32[4,128,128]{2,1,0:T(8,128)S(1)} %fusion.diag_ref, f32[128,128]{1,0:T(8,128)S(1)} %bitcast_select_fusion.right_ref), custom_call_target="tpu_custom_call" | custom-call | tf_op jit(solution)/shard_map/exchange/pallas_call | solution.py:235
  194.8 0.0 copy-start
  194.8 2.0 copy-done
  196.8 0.0 copy-start.1
  196.8 1.0 copy-done.1
  197.9 0.0 copy-start.2
  197.9 0.7 copy-done.2
  198.6 5.0 %gather_fusion.3 = f32[32,64,512]{2,1,0:T(8,128)} fusion(f32[32,64,512]{2,1,0:T(8,128)} %bitcast.16, s32[1024]{0:T(1024)S(1)} %pad_clamp_fusion), kind=kCustom, calls=%fused_computation.3 | custom fusion | bytes 8388736 | tf_op jit(solution)/shard_map/jit(_take)/gather | solution.py:401
  203.6 67.3 %update.1 = (f32[2048,4096]{1,0:T(8,128)}, f32[2048,512]{1,0:T(8,128)}, f32[512,128]{1,0:T(8,128)}, f32[2048,128]{1,0:T(8,128)}) custom-call(f32[512,512]{1,0:T(8,128)} %copy-done.1, f32[512,128]{1,0:T(8,128)} %copy-done.2, f32[8,8,64,512]{3,2,1,0:T(8,128)} %bitcast.21, f32[2048,512]{1,0:T(8,128)} %bitcast.19, f32[2048,4096]{1,0:T(8,128)} %kernel_ref.1, ...), custom_call_target="tpu_custom_call" | custom-call | tf_op jit(solution)/shard_map/update/pallas_call | solution.py:331
  (3 shorter events, 0.0 us)
Async XLA Ops:
  194.8 2.0 copy-start
  196.8 1.1 copy-start.1
  197.9 0.7 copy-start.2
